TPU v7x, 512 devices: a whole 4x8x8 slice. The times are simulated.
512 devices in a mesh: seq: 16 (over x, y_hi, core), fsdp: 8 (over z), chan: 4 (over y_lo).
Axes of the slice: x: 4, y: 8 (y_hi: 2, y_lo: 4; y = y_hi * 4 + y_lo), z: 8, core: 2. Of those that a mesh axis runs over, the one named last changes fastest.
Arguments:
- tokens: bfloat16 [8192, 8192], P('seq', ('fsdp', 'chan')), may hold values from -600 to 600, as said below
- norm_gain: float32 [8192], replicated, may hold values from 0.1 to 1.9
- w_feat: bfloat16 [8192, 3, 4096], P('seq', None, ('fsdp', 'chan')), may hold values from -0.0625 to 0.0625
- pre_taps: float32 [3, 3, 4096], P(None, None, ('fsdp', 'chan')), may hold values from -2.5 to 2.5
- inner_taps: float32 [7, 4096], P(None, ('fsdp', 'chan')), may hold values from -2.5 to 2.5
- w_out: bfloat16 [4096, 8192], P('seq', ('fsdp', 'chan')), may hold values from -0.09375 to 0.09375
Outputs:
- mixed: bfloat16 [8192, 8192], P('seq', ('fsdp', 'chan'))
Inputs may be any that keep to these rules, and one draw needn't show every extreme that they name: `tokens`: finite activations.
All inputs are finite; a program needn't handle non-finite values.
Results may differ from a plain program's by a relative error of at most 0.0085.
Values may be sent and summed in bfloat16 or wider, within the bound.
A program may use at most 64 MiB of HBM per device.

v0:
```python
import jax
import jax.numpy as jnp
from jax import lax
from jax.sharding import PartitionSpec as P


def passed_along(value, axis, steps):
    count = lax.axis_size(axis)
    first, last = (max(0, -steps), min(count, count - steps))
    return lax.ppermute(value, axis, [(source, source + steps) for source in range(first, last)])


def short_conv(extended, tap_table, length_out):
    width_taps = tap_table.shape[0]
    result = jnp.zeros((length_out,) + extended.shape[1:], jnp.float32)
    for lag in range(width_taps):
        begin = width_taps - 1 - lag
        result = result + tap_table[lag] * extended[begin : begin + length_out].astype(jnp.float32)
    return result


def on_device(tokens, norm_gain, w_feat, pre_taps, inner_taps, w_out):
    gathered = lax.all_gather(tokens, ("fsdp", "chan"), axis=1, tiled=True)
    slab_len = gathered.shape[0]
    local_ch = w_feat.shape[2]
    widened = gathered.astype(jnp.float32)
    row_scale = lax.rsqrt(jnp.mean(widened * widened, axis=1, keepdims=True) + 1e-06)
    normed = (widened * row_scale * norm_gain).astype(jnp.bfloat16)
    panel_piece = lax.all_gather(w_feat, "seq", axis=0, tiled=True)
    columns = normed
    flat_piece = panel_piece.reshape(panel_piece.shape[0], 3 * local_ch)
    accum = jnp.dot(columns, flat_piece, preferred_element_type=jnp.float32)
    features = accum.astype(jnp.bfloat16).reshape(slab_len, 3, local_ch)
    edge_rows = passed_along(features[slab_len - 2 :], "seq", 1)
    filtered = short_conv(jnp.concatenate([edge_rows, features], axis=0), pre_taps, slab_len)
    key_value = filtered[:, 1] * filtered[:, 2]
    edge_kv = passed_along(key_value[slab_len - 6 :], "seq", 1)
    inner_out = short_conv(jnp.concatenate([edge_kv, key_value], axis=0), inner_taps, slab_len)
    query_part = filtered[:, 0]
    gated = (query_part * inner_out).astype(jnp.bfloat16)
    gated_rows = lax.all_gather(gated, ("fsdp", "chan"), axis=1, tiled=True)
    columns = gated_rows
    result = jnp.dot(
        columns,
        lax.all_gather(w_out, "seq", axis=0, tiled=True),
        preferred_element_type=jnp.float32,
    )
    return result.astype(jnp.bfloat16)


def solution(mesh):
    in_specs = (
        P("seq", ("fsdp", "chan")),
        P(),
        P("seq", None, ("fsdp", "chan")),
        P(None, None, ("fsdp", "chan")),
        P(None, ("fsdp", "chan")),
        P("seq", ("fsdp", "chan")),
    )
    out_specs = P("seq", ("fsdp", "chan"))
    return jax.shard_map(
        on_device, mesh=mesh, in_specs=in_specs, out_specs=out_specs, check_vma=False
    )
```

profile of v0, /device:TPU:6, one launch (start us, length us, event | category | flops | bytes accessed | tf_op | source)
XLA Modules:
  0.0 581.3 jit_solution(5924779002329208063)
XLA Ops:
  6.5 0.7 all-gather.5.cloned.1.call-update
  7.3 0.0 all-gather.7.cloned.1.call-start
  7.3 1.9 copy.8
  9.2 0.0 all-gather.7.cloned.1.call-update
  9.3 0.0 all-gather.11.cloned.1.call-start
  9.3 0.7 all-gather.11.cloned.1.call-update
  10.0 0.0 all-gather.9.cloned.1.call-start
  10.0 0.7 slice_bitcast_fusion.4
  10.8 222.5 %all-gather.5.cloned.1.call-done = bf16[512,8192]{1,0:T(8,128)(2,1)} async-done(((bf16[512,256]{1,0:T(8,128)(2,1)}), bf16[512,8192]{1,0:T(8,128)(2,1)}) %all-gather.5.cloned.1.call-update) | async-done | bytes 8388624 | tf_op jit(solution)/shard_map/all_gather | solution.py:23
  233.3 5.1 fusion
  238.4 92.9 %all-gather.7.cloned.1.call-done = bf16[8192,3,128]{0,2,1:T(8,128)(2,1)} async-done(((bf16[512,3,128]{0,2,1:T(8,128)(2,1)}), bf16[8192,3,128]{0,2,1:T(8,128)(2,1)}) %all-gather.7.cloned.1.call-update) | async-done | bytes 6291472 | tf_op jit(solution)/shard_map/all_gather | solution.py:29
  331.3 9.7 %fusion.7 = bf16[512,384]{1,0:T(8,128)(2,1)S(1)} fusion(bf16[8192,384]{0,1:T(8,128)(2,1)} %bitcast.36, bf16[512,8192]{1,0:T(8,128)(2,1)} %all-gather.5.cloned.1.call-done, f32[8192]{0:T(1024)S(1)} %copy-done.1, f32[512]{0:T(512)S(1)} %add_rsqrt_fusion), kind=kOutput, calls=%fused_computation.8 | convolution fusion | flops 3238199296 | bytes 15108096 | tf_op jit(solution)/shard_map/dot_general | solution.py:32
  341.1 0.2 copy.11
  341.2 2.2 collective-permute-start
  343.4 0.2 copy.9
  343.6 8.4 %collective-permute-done = bf16[2,3,128]{0,2,1:T(8,128)(2,1)S(1)} collective-permute-done((bf16[2,3,128]{0,2,1:T(8,128)(2,1)S(1)}, bf16[2,3,128]{0,2,1:T(8,128)(2,1)S(1)}, u32[]{:S(2)}, u32[]{:S(2)}) %collective-permute-start) | collective-permute-done | bytes 1568 | tf_op jit(solution)/shard_map/ppermute | solution.py:10
  352.0 0.6 multiply_add_fusion
  352.6 0.1 slice_bitcast_fusion.1
  352.7 1.9 collective-permute-start.1
  354.7 8.5 %collective-permute-done.1 = f32[6,128]{0,1:T(8,128)S(1)} collective-permute-done((f32[6,128]{0,1:T(8,128)S(1)}, f32[6,128]{0,1:T(8,128)S(1)}, u32[]{:S(2)}, u32[]{:S(2)}) %collective-permute-start.1) | collective-permute-done | bytes 3104 | tf_op jit(solution)/shard_map/ppermute | solution.py:10
  363.2 1.4 fusion.16
  364.6 34.6 %all-gather.11.cloned.1.call-done = bf16[4096,256]{1,0:T(8,128)(2,1)} async-done(((bf16[256,256]{1,0:T(8,128)(2,1)}), bf16[4096,256]{1,0:T(8,128)(2,1)}) %all-gather.11.cloned.1.call-update) | async-done | bytes 2097168 | tf_op jit(solution)/shard_map/all_gather | solution.py:45
  399.1 170.8 %all-gather.9.cloned.1.call-done = bf16[512,4096]{0,1:T(8,128)(2,1)} async-done(((bf16[512,128]{0,1:T(8,128)(2,1)}), bf16[512,4096]{0,1:T(8,128)(2,1)}) %all-gather.9.cloned.1.call-update) | async-done | bytes 4194320 | tf_op jit(solution)/shard_map/all_gather | solution.py:41
  570.0 4.9 convolution_convert_fusion
  (11 shorter events, 0.1 us)
Async XLA Ops:
  6.5 324.8 %copy-start.1 = (f32[8192]{0:T(1024)S(1)}, f32[8192]{0:T(1024)}, u32[]{:S(2)}) copy-start(f32[8192]{0:T(1024)} %param.7) | copy-start | bytes 98308
  6.5 226.8 %all-gather.5.cloned.1.call-start = ((), (), s32[]{:S(2)}) async-start(), calls=%async_computation | async-start | bytes 8650752 | tf_op jit(solution)/shard_map/all_gather | solution.py:23
  7.3 324.1 %all-gather.7.cloned.1.call-start = ((), (), s32[]{:S(2)}) async-start(), calls=%async_computation.1 | async-start | bytes 6684672 | tf_op jit(solution)/shard_map/all_gather | solution.py:29
  9.3 389.9 %all-gather.11.cloned.1.call-start = ((), (), s32[]{:S(2)}) async-start(), calls=%async_computation.3 | async-start | bytes 2228224 | tf_op jit(solution)/shard_map/all_gather | solution.py:45
  10.0 560.0 %all-gather.9.cloned.1.call-start = ((), (), s32[]{:S(2)}) async-start(), calls=%async_computation.2 | async-start | bytes 4325376 | tf_op jit(solution)/shard_map/all_gather | solution.py:41
  331.3 12.1 %copy-start = (f32[7,128]{1,0:T(8,128)S(1)}, f32[7,128]{1,0:T(8,128)}, u32[]{:S(2)}) copy-start(f32[7,128]{1,0:T(8,128)} %param.10) | copy-start | bytes 10756
  341.2 10.8 %collective-permute-start = (bf16[2,3,128]{0,2,1:T(8,128)(2,1)S(1)}, bf16[2,3,128]{0,2,1:T(8,128)(2,1)S(1)}, u32[]{:S(2)}, u32[]{:S(2)}) collective-permute-start(bf16[2,3,128]{0,2,1:T(8,128)(2,1)S(1)} %bitcast.35), channel_id=1, source_target_pairs={{0,32},{32,64},{64,96},{96,128},{128,160},{160,192},{192,224},{224... | collective-permute-start | bytes 4616 | tf_op jit(solution)/shard_map/ppermute | solution.py:10
  352.7 10.5 %collective-permute-start.1 = (f32[6,128]{0,1:T(8,128)S(1)}, f32[6,128]{0,1:T(8,128)S(1)}, u32[]{:S(2)}, u32[]{:S(2)}) collective-permute-start(f32[6,128]{0,1:T(8,128)S(1)} %slice_bitcast_fusion.1), channel_id=1, source_target_pairs={{0,32},{32,64},{64,96},{96,128},{128,160},{160,192},{192,224},{224... | collective-permute-start | bytes 9224 | tf_op jit(solution)/shard_map/ppermute | solution.py:10
Sparse Core Ops, SparseCore 0:
  9.4 223.8 all-gather.4
  236.4 94.8 all-gather.6
  334.6 64.5 all-gather.10
  401.1 168.8 all-gather.8
where the time goes:
time: 582 us; the launch traced here: 581 us
  waiting for transfers between devices  539 us (93%)
  matrix products  14.6 us (3%)
  between operations  13.2 us (2%)
  other arithmetic  7.11 us (1%)
    all_gather x1, waiting for transfers between devices, on_device(): gathered = lax.all_gather(tokens, ('fsdp', 'chan'), axis=1, tiled=True)  223 us
    all_gather x1, waiting for transfers between devices, on_device(): gated_rows = lax.all_gather(gated, ('fsdp', 'chan'), axis=1, tiled=True)  171 us
    all_gather x1, waiting for transfers between devices, on_device(): panel_piece = lax.all_gather(w_feat, 'seq', axis=0, tiled=True)  92.9 us
    all_gather x1, waiting for transfers between devices, on_device(): lax.all_gather(w_out, 'seq', axis=0, tiled=True)  34.6 us
    ppermute x2, waiting for transfers between devices, passed_along(): lax.ppermute(value, axis, [(source, source + steps) for source in range(f...  16.9 us
  transfers between devices with their start and end apart: 6, of which 6 were waited for; matrix products, arithmetic and copies ran while one was open for 3% of the time, Pallas kernels for 0%

commit v1 on v0

v1 whole, which is shorter than its diff:
```python
import heapq

import jax
import jax.numpy as jnp
from jax import lax
from jax.experimental import pallas as pl
from jax.experimental.pallas import tpu as pltpu
from jax.sharding import PartitionSpec as P

MESH = pl.DeviceIdType.MESH
F32, BF16 = jnp.float32, jnp.bfloat16
SLAB, HALO, EXT = 512, 16, 528
NSEM = 160
TOKEN_ROWS = ((272, 256), (0, 272))
GATED_ROWS = ((272, 240), (0, 272))


def body(
    tok, gain, wf, pre, inner, wo, out,
    xr, xn, panel, panel_out, acc, psend, precv, feats, kv, ssq, ssend, srecv, gat, acc2, osend, orecv,
    send_sem, recv_sem, local_sem,
):
    s, z, c = lax.axis_index("seq"), lax.axis_index("fsdp"), lax.axis_index("chan")
    kappa = lax.rem(c, 2)
    high = c // 2
    c1 = c + 1 - 2 * kappa
    c2 = lax.rem(c + 2, 4)
    core = lax.rem(s, 2)
    y_hi = lax.rem(s // 2, 2)
    zp, zm = lax.rem(z + 1, 8), lax.rem(z + 7, 8)
    dev_zp, dev_zm = (s, zp, c), (s, zm, c)
    dev_c1, dev_c2 = (s, z, c1), (s, z, c2)
    s_yh = s + 2 - 4 * y_hi
    dev_yh = (s_yh, z, c)
    dev_xp, dev_xm = (lax.rem(s + 4, 16), z, c), (lax.rem(s + 12, 16), z, c)
    s_sib = s + 1 - 2 * core
    dev_sib = (s_sib, z, c)
    dev_next, dev_prev = (lax.rem(s + 1, 16), z, c), (lax.rem(s + 15, 16), z, c)
    peers = (dev_zp, dev_zm, dev_c1, dev_c2, dev_yh, dev_xp, dev_xm, dev_sib, dev_next, dev_prev)

    barrier = pltpu.get_barrier_semaphore()
    for dev in peers:
        pl.semaphore_signal(barrier, inc=1, device_id=dev, device_id_type=MESH)
    pl.semaphore_wait(barrier, len(peers))

    started, count = [], [0]

    def send(src, dst, dev):
        k = count[0]
        count[0] += 1
        copy = pltpu.make_async_remote_copy(src, dst, send_sem.at[k], recv_sem.at[k], device_id=dev, device_id_type=MESH)
        copy.start()
        started.append(copy)
        return k

    def arrived(k, landed):
        pltpu.make_async_remote_copy(
            landed, landed, send_sem.at[k], recv_sem.at[k], device_id=dev_zp, device_id_type=MESH
        ).wait_recv()

    def block_of(steps, hi):
        return 2 * lax.rem(z + steps + 8, 8) + hi

    done = {}

    def ring(view, begin, hop, key, own_hi, far_right):
        own = view(block_of(0, own_hi))
        right = send(own, own, dev_zp)
        left = send(own, own, dev_zm)
        for step in (1, 2, 3, 4):
            yield begin + hop * step
            take_right = step < 4 or far_right
            take_left = step < 4 or not far_right
            if take_right:
                landed = view(block_of(-step, own_hi))
                arrived(right, landed)
                if step < 3 or (step == 3 and far_right):
                    right = send(landed, landed, dev_zp)
            if take_left:
                landed = view(block_of(step, own_hi))
                arrived(left, landed)
                if step < 3 or (step == 3 and not far_right):
                    left = send(landed, landed, dev_zm)
        done[key] = True

    def gather(view, begin, hop, other, key):
        mine = view(block_of(0, high))
        k = send(mine, mine, dev_c2)
        first = ring(view, begin, hop, key + ("a",), high, True)
        t_first = next(first)
        t_other = begin + other
        second = None
        while first is not None or second is not None or t_other is not None:
            options = [t for t in (t_first, t_other) if t is not None]
            if second is not None:
                options.append(t_second)
            now = min(options)
            yield now
            if t_other is not None and now == t_other:
                arrived(k, view(block_of(0, 1 - high)))
                second = ring(view, now, hop, key + ("b",), 1 - high, False)
                t_second = next(second)
                t_other = None
            elif first is not None and now == t_first:
                t_first = next(first, None)
                if t_first is None:
                    first = None
            else:
                t_second = next(second, None)
                if t_second is None:
                    second = None
        done[key] = True

    def weights(src, dst, rows, cols, begin, scale, key):
        def place(block, part):
            return dst.at[pl.ds(pl.multiple_of(block * rows, rows), rows), pl.ds(part * cols, cols)]

        def whole(block):
            return dst.at[pl.ds(pl.multiple_of(block * rows, rows), rows), :]

        swap = send(src.at[pl.ds(pl.multiple_of((1 - kappa) * rows, rows), rows), :], place(s, 1), dev_c1)
        held = src.at[pl.ds(pl.multiple_of(kappa * rows, rows), rows), :]
        local = pltpu.make_async_copy(held, place(s, 0), local_sem.at[0 if key == "w" else 1])
        local.start()
        far = [send(held, place(s, 0), dev_yh)]
        chains = []

        def chain(block, part, src_ref, at):
            right = send(src_ref, place(block, part), dev_xp)
            left = send(src_ref, place(block, part), dev_xm)
            yield at + 8 * scale
            landed = place(lax.rem(block + 12, 16), part)
            arrived(right, landed)
            if part == 0:
                last = send(landed, landed, dev_xp)
            landed = place(lax.rem(block + 4, 16), part)
            arrived(left, landed)
            if part == 1:
                last = send(landed, landed, dev_xm)
            yield at + 16 * scale
            arrived(last, place(lax.rem(block + 8, 16), part))

        order = 0

        def add(gen):
            nonlocal order
            t = next(gen, None)
            if t is not None:
                heapq.heappush(chains, (t, order, gen))
                order += 1

        def swapped():
            yield begin + 6 * scale
            arrived(swap, place(s, 1))
            far.append(send(place(s, 1), place(s, 1), dev_yh))
            add(chain(s, 1, place(s, 1), begin + 6 * scale))
            yield begin + 14 * scale
            arrived(far[0], place(s_yh, 0))
            add(chain(s_yh, 0, place(s_yh, 0), begin + 14 * scale))
            yield begin + 24 * scale
            arrived(far[1], place(s_yh, 1))
            add(chain(s_yh, 1, place(s_yh, 1), begin + 24 * scale))

        add(chain(s, 0, held, begin))
        add(swapped())
        while chains:
            t, _, gen = heapq.heappop(chains)
            yield t
            add(gen)
        local.wait()
        mine, copies = [], []
        for i in range(8):
            block = 2 * i + core
            copies.append(send(whole(block), whole(block), dev_sib))
        yield begin + 42 * scale
        for i, k in enumerate(copies):
            arrived(k, whole(2 * i + 1 - core))
        done[key] = True

    def needs(*keys):
        return all(key in done for key in keys)

    def scaled(chunk):
        r0, nr = TOKEN_ROWS[chunk]
        gains = [gain[:, pl.ds(pl.multiple_of(b * 512 + kappa * 256, 256), 256)] for b in range(16)]

        @pl.loop(0, nr // 16)
        def _(i):
            rows = pl.ds(pl.multiple_of(r0 + i * 16, 16), 16)
            total = jnp.zeros((16, 128), F32)
            for b in range(16):
                x = xr[b, rows, :].astype(F32)
                total = total + x[:, :128] * x[:, :128] + x[:, 128:] * x[:, 128:]
                xn[rows, b * 256 : (b + 1) * 256] = (x * gains[b]).astype(BF16)
            ssq[rows, :] = total

    def squares(chunk):
        r0, nr = TOKEN_ROWS[chunk]
        part = lax.dot_general(
            jnp.ones((8, 128), F32), ssq[r0 : r0 + nr, :], (((1,), (1,)), ((), ())),
            precision=lax.Precision.HIGHEST, preferred_element_type=F32,
        )
        ssend[chunk, :, 0:nr] = part

    def product(chunk, half):
        r0, nr = TOKEN_ROWS[chunk]
        cols = slice(half * 384, half * 384 + 384)
        acc[r0 : r0 + nr, :] = jnp.dot(xn[r0 : r0 + nr, 0:1024], panel[0:1024, cols], preferred_element_type=F32)

        @pl.loop(1, 4)
        def _(k):
            depth = pl.ds(pl.multiple_of(k * 1024, 1024), 1024)
            acc[r0 : r0 + nr, :] += jnp.dot(xn[r0 : r0 + nr, depth], panel[depth, cols], preferred_element_type=F32)

    def combine(chunk):
        r0, nr = TOKEN_ROWS[chunk]
        both = ssend[chunk, :, 0:nr] + srecv[chunk, :, 0:nr]
        eye = (lax.broadcasted_iota(jnp.int32, (nr, nr), 0) == lax.broadcasted_iota(jnp.int32, (nr, nr), 1)).astype(F32)
        column = lax.dot_general(
            eye, both, (((1,), (1,)), ((), ())), precision=lax.Precision.HIGHEST, preferred_element_type=F32
        )[:, 0:1]
        scale = lax.rsqrt(column * (1.0 / 8192.0) + 1e-06)
        if chunk == 1:
            row = lax.broadcasted_iota(jnp.int32, (nr, 1), 0)
            scale = jnp.where((row < HALO) & (s == 0), 0.0, scale)
        total = acc[r0 : r0 + nr, :] + precv[r0 : r0 + nr, :].astype(F32)
        feats[r0 : r0 + nr, :] = total * scale

    def gates(chunk):
        t0, nr = GATED_ROWS[chunk]
        e0 = t0 + HALO

        def filtered(i, begin, rows):
            value = jnp.zeros((rows, 128), F32)
            for lag in range(3):
                value = value + pre[lag, i : i + 1, :] * feats[begin - lag : begin - lag + rows, i * 128 : i * 128 + 128]
            return value

        kv[e0 - 8 : e0 + nr, :] = filtered(1, e0 - 8, nr + 8) * filtered(2, e0 - 8, nr + 8)
        value = jnp.zeros((nr, 128), F32)
        for lag in range(7):
            value = value + inner[lag : lag + 1, :] * kv[e0 - lag : e0 - lag + nr, :]
        block = pl.multiple_of((2 * z + high) * 128, 128)
        gat[t0 : t0 + nr, pl.ds(block, 128)] = (filtered(0, e0, nr) * value).astype(BF16)

    def product_out(chunk):
        t0, nr = GATED_ROWS[chunk]
        acc2[t0 : t0 + nr, :] = jnp.dot(gat[t0 : t0 + nr, 0:1024], panel_out[0:1024, :], preferred_element_type=F32)
        acc2[t0 : t0 + nr, :] += jnp.dot(gat[t0 : t0 + nr, 1024:2048], panel_out[1024:2048, :], preferred_element_type=F32)

    def x_view(chunk):
        r0, nr = TOKEN_ROWS[chunk]
        return lambda block: xr.at[block, pl.ds(r0, nr), :]

    def g_view(chunk):
        t0, nr = GATED_ROWS[chunk]
        return lambda block: gat.at[pl.ds(t0, nr), pl.ds(pl.multiple_of(block * 128, 128), 128)]

    ssend[...] = jnp.zeros_like(ssend)
    mine = block_of(0, high)
    xr[mine, HALO:EXT, :] = tok[...]
    halo_k = send(tok.at[pl.ds(SLAB - HALO, HALO), :], xr.at[mine, pl.ds(0, HALO), :], dev_next)

    def stage_one(chunk, begin, compute_at):
        if chunk == 1:
            yield begin
            arrived(halo_k, xr.at[mine, pl.ds(0, HALO), :])
        yield from gather(x_view(chunk), begin, 5.5, 8, ("x", chunk))
        yield compute_at
        scaled(chunk)
        squares(chunk)
        while "w" not in done:
            yield compute_at
            compute_at += 1
        yield compute_at
        r0, nr = TOKEN_ROWS[chunk]
        product(chunk, 1)
        psend[r0 : r0 + nr, :] = acc[r0 : r0 + nr, :].astype(BF16)
        k1 = send(psend.at[pl.ds(r0, nr), :], precv.at[pl.ds(r0, nr), :], dev_c1)
        k2 = send(ssend.at[chunk], srecv.at[chunk], dev_c1)
        yield compute_at + 2
        product(chunk, 0)
        yield compute_at + 6
        arrived(k1, precv.at[pl.ds(r0, nr), :])
        arrived(k2, srecv.at[chunk])
        combine(chunk)
        gates(chunk)
        at = compute_at + 8
        yield from gather(g_view(chunk), at, 2.6, 4, ("g", chunk))
        yield at + 14
        while "wo" not in done:
            at += 1
            yield at
        product_out(chunk)
        t0, ng = GATED_ROWS[chunk]
        osend[t0 : t0 + ng, :] = acc2[t0 : t0 + ng, 256:512].astype(BF16)
        k3 = send(osend.at[pl.ds(t0, ng), :], orecv.at[pl.ds(t0, ng), :], dev_c1)
        yield at + 19
        arrived(k3, orecv.at[pl.ds(t0, ng), :])
        out[t0 : t0 + ng, :] = (acc2[t0 : t0 + ng, 0:256] + orecv[t0 : t0 + ng, :].astype(F32)).astype(BF16)

    streams = []
    gens = [
        (0, stage_one(0, 0, 28)),
        (0.1, weights(wf, panel, 256, 384, 0, 1.0, "w")),
        (3, stage_one(1, 6, 45)),
        (20, weights(wo, panel_out, 128, 256, 20, 0.6, "wo")),
    ]
    for i, (t, gen) in enumerate(gens):
        heapq.heappush(streams, (t, i, gen))
    while streams:
        _, i, gen = heapq.heappop(streams)
        t = next(gen, None)
        if t is not None:
            heapq.heappush(streams, (t, i, gen))
    for copy in started:
        copy.wait_send()


def on_device(tokens, norm_gain, w_feat, pre_taps, inner_taps, w_out):
    vmem = pl.BlockSpec(memory_space=pltpu.VMEM)
    return pl.pallas_call(
        body,
        out_shape=jax.ShapeDtypeStruct((SLAB, 256), BF16),
        in_specs=[vmem] * 6,
        out_specs=vmem,
        scratch_shapes=[
            pltpu.VMEM((16, EXT, 256), BF16),
            pltpu.VMEM((EXT, 4096), BF16),
            pltpu.VMEM((4096, 768), BF16),
            pltpu.VMEM((2048, 512), BF16),
            pltpu.VMEM((EXT, 384), F32),
            pltpu.VMEM((EXT, 384), BF16),
            pltpu.VMEM((EXT, 384), BF16),
            pltpu.VMEM((EXT, 384), F32),
            pltpu.VMEM((EXT, 128), F32),
            pltpu.VMEM((EXT, 128), F32),
            pltpu.VMEM((2, 8, 384), F32),
            pltpu.VMEM((2, 8, 384), F32),
            pltpu.VMEM((SLAB, 2048), BF16),
            pltpu.VMEM((SLAB, 512), F32),
            pltpu.VMEM((SLAB, 256), BF16),
            pltpu.VMEM((SLAB, 256), BF16),
            pltpu.SemaphoreType.DMA((NSEM,)),
            pltpu.SemaphoreType.DMA((NSEM,)),
            pltpu.SemaphoreType.DMA((2,)),
        ],
        compiler_params=pltpu.CompilerParams(
            collective_id=0, has_side_effects=True, vmem_limit_bytes=56 * 1024 * 1024
        ),
    )(tokens, norm_gain.reshape(1, 8192), w_feat.reshape(512, 384), pre_taps, inner_taps, w_out)


def solution(mesh):
    in_specs = (
        P("seq", ("fsdp", "chan")),
        P(),
        P("seq", None, ("fsdp", "chan")),
        P(None, None, ("fsdp", "chan")),
        P(None, ("fsdp", "chan")),
        P("seq", ("fsdp", "chan")),
    )
    out_specs = P("seq", ("fsdp", "chan"))
    return jax.shard_map(
        on_device, mesh=mesh, in_specs=in_specs, out_specs=out_specs, check_vma=False
    )
```

time: 582 us -> 135 us (0.23)
  the two profiles are of different devices: /device:TPU:6 before, /device:TPU:1 now
where the time goes in v1:
time: 135 us
  Pallas kernels  131 us (97%)
  local copies, waits for them, and re-layouts  3.75 us (3%)
    pallas_call x1, Pallas kernels, on_device(): pl.pallas_call(body, out_shape=jax.ShapeDtypeStruct((SLAB, 256), BF16), i...  131 us
    unnamed x2, local copies, waits for them, and re-layouts  2.83 us

profile of v1, /device:TPU:1, one launch (start us, length us, event | category | flops | bytes accessed | tf_op | source)
XLA Modules:
  0.0 135.2 jit_solution(11874548327103378353)
XLA Ops:
  0.0 1.2 copy.8
  1.2 0.9 copy.9.wf
  2.1 131.4 %shard_map.64 = bf16[512,256]{1,0:T(8,128)(2,1)} custom-call(bf16[512,256]{1,0:T(8,128)(2,1)} %tok.1, f32[1,8192]{1,0:T(1,128)} %bitcast.3, bf16[512,384]{1,0:T(8,128)(2,1)} %copy.9.wf, f32[3,3,128]{2,1,0:T(4,128)} %pre.1, f32[7,128]{1,0:T(8,128)} %inner.1, bf16[256,256]{1,0:T(8,128)(2,1)} %wo.1), custom_call_target="tpu_custom_call" | custom-call | tf_op jit(solution)/shard_map/pallas_call | solution.py:322
  133.5 1.7 %copy.11 = bf16[512,256]{1,0:T(8,128)(2,1)} copy(bf16[512,256]{1,0:T(8,128)(2,1)} %shard_map.64) | data formatting | bytes 524288

commit v2 on v0

v2 whole, which is shorter than its diff:
```python
import jax
import jax.numpy as jnp
from jax import lax
from jax.experimental import pallas as pl
from jax.experimental.pallas import tpu as pltpu
from jax.sharding import PartitionSpec as P

MESH = pl.DeviceIdType.MESH
F32, BF16 = jnp.float32, jnp.bfloat16
SLAB, HALO, EXT = 512, 16, 528
N_SEND, N_RECV = 40, 211
TOKEN_ROWS = ((384, 512), (256, 384), (128, 256), (0, 128))
CHUNKS = ((384, 512), (256, 384), (128, 256), (0, 128))
RATE = {"z+": 45.0, "z-": 45.0, "x+": 45.0, "x-": 45.0, "y": 22.5, "c1": 45.0, "core": 400.0}
LATENCY = 2.8
FAIR = ("y", "c1")
TOKEN_BEGIN = (0.0, 1.6, 5.3, 26.8)
RIGHT, LEFT = {(1, 0): [(2, 0)], (2, 0): [(3, 0)], (3, 0): [(4, 0)]}, {(-1, 0): [(-2, 0)], (-2, 0): [(-3, 0)]}
OTHER = {(1, 1): [(2, 1)], (2, 1): [(3, 1)], (-1, 1): [(-2, 1)], (-2, 1): [(-3, 1)], (-3, 1): [(-4, 1)]}
SKIP = {
    (1, 0): [(3, 0), (2, 0)], (3, 0): [(4, 0)], (-1, 0): [(-2, 0)], (-2, 0): [(-3, 0)],
    (1, 1): [(2, 1)], (2, 1): [(3, 1)], (-1, 1): [(-3, 1), (-2, 1)], (-3, 1): [(-4, 1)],
}
OTHER_Y = {(1, 1): [(2, 1)], (2, 1): [(3, 1)], (-1, 1): [(-2, 1)], (-2, 1): [(-3, 1)], (4, 0): [(4, 1)]}
TREES = {
    "ring": {(0, 0): [(0, 1), (1, 0), (-1, 0)], (0, 1): [(-1, 1), (1, 1)], **RIGHT, **LEFT, **OTHER},
    "diag": {(0, 0): [(1, 0), (-1, 0), (-1, 1), (1, 1), (0, 1)], **RIGHT, **LEFT, **OTHER},
    "skip": {(0, 0): [(0, 1), (1, 0), (-1, 0)], (0, 1): [(-1, 1), (1, 1)], **SKIP},
    "fast": {(0, 0): [(1, 0), (-1, 1), (-1, 0), (1, 1), (0, 1)], **SKIP},
    "viay": {(0, 0): [(0, 1), (1, 0), (-1, 0)], (0, 1): [(-1, 1), (1, 1)], **RIGHT, **LEFT, **OTHER_Y},
}
TOKEN_TREE = ("ring", "viay", "ring", "skip")
GATED_TREE = ("ring", "diag", "viay", "fast")
WO_BEGIN = 33.0
FAR_AFTER = True
FAR_SPLIT = 2
FAR_DIRECT = True


class Plan:
    def __init__(self):
        self.clock, self.flows, self.landed, self.left = 0.0, [], {}, {}
        self.flags, self.streams, self.order, self.log = set(), [], 0, []

    def spawn(self, gen, rank=0):
        self.order += 1
        self.resume([rank, self.order, gen, None])

    def resume(self, stream):
        stream[3] = next(stream[2], None)
        if stream[3] is not None:
            self.streams.append(stream)

    def start(self, key, link, kib):
        if key is None:
            self.order += 1
            key = -self.order
        self.flows.append([key, link, float(kib)])
        self.clock_to(self.clock + 0.08)

    def busy(self, us):
        self.clock_to(self.clock + us)

    def shares(self):
        total = {}
        for flow in self.flows:
            total.setdefault(flow[1], []).append(flow)
        share = {}
        for link, flows in total.items():
            for i, flow in enumerate(flows):
                share[flow[0]] = RATE[link] / len(flows) if link in FAIR else RATE[link] * (i == 0)
        return share

    def clock_to(self, until):
        while True:
            share = self.shares()
            ends = [flow[2] / share[flow[0]] for flow in self.flows if share[flow[0]]]
            step = min(ends + [until - self.clock])
            for flow in self.flows:
                flow[2] -= step * share[flow[0]]
            self.clock += step
            for flow in [f for f in self.flows if f[2] <= 1e-6]:
                self.flows.remove(flow)
                self.left[flow[0]] = self.clock + 0.3
                self.landed[flow[0]] = self.clock + LATENCY
            if self.clock >= until - 1e-9:
                return

    def when(self, need):
        if isinstance(need, float):
            return need
        if isinstance(need, str):
            return 0.0 if need in self.flags else None
        if isinstance(need, tuple):
            return self.left.get(need[1])
        return self.landed.get(need)

    def run(self):
        while self.streams:
            best = None
            for stream in self.streams:
                times = [self.when(need) for need in stream[3]]
                if any(t is None for t in times):
                    continue
                at = max(times + [0.0])
                ready = (max(at, self.clock), stream[0], at, stream[1])
                if best is None or ready < best[0]:
                    best = (ready, stream)
            share = self.shares()
            ends = [self.clock + flow[2] / share[flow[0]] for flow in self.flows if share[flow[0]]]
            if best is not None and (not ends or best[0][0] <= min(ends)):
                self.clock_to(max(best[0][0], self.clock))
                self.streams.remove(best[1])
                self.resume(best[1])
            else:
                self.clock_to(min(ends))


def body(
    tok_hbm, gain_hbm, w3, pre_hbm, inner_hbm, wo_hbm, out_hbm,
    gain, pre, inner, wo, out, wf, xr, xn, panel, panel_out, acc, psend, precv, feats, edge, kv, ssq, ssend, srecv, gat, acc2, osend, orecv,
    send_sem, recv_sem, local_sem, load_sem, store_sem,
):
    s, z, c = lax.axis_index("seq"), lax.axis_index("fsdp"), lax.axis_index("chan")
    kappa = lax.rem(c, 2)
    high = c // 2
    c1 = c + 1 - 2 * kappa
    c2 = lax.rem(c + 2, 4)
    core = lax.rem(s, 2)
    y_hi = lax.rem(s // 2, 2)
    s_yh = s + 2 - 4 * y_hi
    s_sib = s + 1 - 2 * core
    zp, zm = (s, lax.rem(z + 1, 8), c), (s, lax.rem(z + 7, 8), c)
    dev_c1, dev_c2 = (s, z, c1), (s, z, c2)
    dev_yh, dev_yh1 = (s_yh, z, c), (s_yh, z, c1)
    xp, xm = (lax.rem(s + 4, 16), z, c), (lax.rem(s + 12, 16), z, c)
    xf = (lax.rem(s + 8, 16), z, c)
    dev_sib = (s_sib, z, c)
    dev_next, dev_prev = (lax.rem(s + 1, 16), z, c), (lax.rem(s + 15, 16), z, c)
    peers = (zp, zm, dev_c1, dev_c2, dev_yh, dev_yh1, xp, xm, xf, dev_sib, dev_next, dev_prev)

    barrier = pltpu.get_barrier_semaphore()
    for dev in peers:
        pl.semaphore_signal(barrier, inc=1, device_id=dev, device_id_type=MESH)
    loads = [
        pltpu.make_async_copy(src, dst, load_sem.at[i])
        for i, (src, dst) in enumerate(
            [(tok_hbm, xr.at[2 * z + high])]
            + [(w3.at[i], wf.at[:, pl.ds(i * 128, 128)]) for i in range(3)]
            + [(wo_hbm, wo), (gain_hbm, gain), (pre_hbm, pre), (inner_hbm, inner)]
        )
    ]
    for load in loads:
        load.start()
    feats[0:8, :] = jnp.zeros((8, 384), F32)
    ssend[...] = jnp.zeros_like(ssend)
    pl.semaphore_wait(barrier, len(peers))
    for load in loads:
        load.wait()

    plan = Plan()
    started, flying = [], []

    def send(src, dst, dev, link, kib):
        k = len(started)
        if len(flying) < N_SEND:
            slot = len(flying)
        else:
            old, slot = flying.pop(0)
            sent(old)
        copy = pltpu.make_async_remote_copy(src, dst, send_sem.at[slot], recv_sem.at[k], device_id=dev, device_id_type=MESH)
        copy.start()
        started.append([copy, False])
        flying.append((k, slot))
        plan.start(k, link, kib)
        return k

    def sent(k):
        if not started[k][1]:
            started[k][0].wait_send()
            started[k][1] = True

    def arrived(k, landed):
        pltpu.make_async_remote_copy(
            landed, landed, send_sem.at[0], recv_sem.at[k], device_id=zp, device_id_type=MESH
        ).wait_recv()

    def block_of(steps, hi):
        return 2 * lax.rem(z + steps + 8, 8) + hi

    def gather(view, kib, use, flag, tree):
        count = [0]

        def holder(node):
            return block_of(-node[0], high if node[1] == 0 else 1 - high)

        def pass_on(node):
            ref = view(holder(node))
            for child in tree.get(node, ()):
                steps, turn = child[0] - node[0], child[1] != node[1]
                dev = (s, lax.rem(z + steps + 8, 8), c2 if turn else c)
                link = "z+" if steps > 0 else "z-"
                if turn and steps:
                    plan.start(None, link, kib)
                k = send(ref, ref, dev, "y" if turn else link, kib * (1 if turn else abs(steps)))
                plan.spawn(take(child, k))
            use(holder(node))
            count[0] += 1
            if count[0] == 16:
                plan.flags.add(flag)

        def take(node, k):
            yield [k]
            arrived(k, view(holder(node)))
            pass_on(node)

        pass_on((0, 0))

    def weights(src, dst, rows, cols, key, sem):
        def place(block, piece):
            part, r0, nr = piece
            return dst.at[pl.ds(pl.multiple_of(block * rows + r0, 16), nr), pl.ds(part * cols, cols)]

        def mine(piece):
            part, r0, nr = piece
            half = kappa if part == 0 else 1 - kappa
            return src.at[pl.ds(pl.multiple_of(half * rows + r0, 16), nr), :]

        def kib(piece):
            return piece[2] * cols * 2 / 1024

        rest = [2 * 16 * rows]
        local = pltpu.make_async_copy(mine((0, 0, rows)), place(s, (0, 0, rows)), sem)

        def to_sibling(base, far, piece, ref):
            k = send(ref, place(lax.rem(base + far, 16), piece), dev_sib, "core", kib(piece))

            def take():
                yield [k]
                arrived(k, place(lax.rem(base + 1 - 2 * core + far, 16), piece))
                rest[0] -= 2 * piece[2]
                if not rest[0]:
                    local.wait()
                    plan.flags.add(key)

            plan.spawn(take(), 1)

        def across(base, piece, ref, direct):
            part = piece[0]
            kr = send(ref, place(base, piece), xp, "x+", kib(piece))
            kl = send(ref, place(base, piece), xm, "x-", kib(piece))
            if direct:
                plan.start(None, "x-", kib(piece))
                kf = send(ref, place(base, piece), xf, "x+", kib(piece))

            def take(k, far, onward, dev, link):
                yield [k]
                ref = place(lax.rem(base + far, 16), piece)
                arrived(k, ref)
                if onward:
                    k = send(ref, ref, dev, link, kib(piece))
                to_sibling(base, far, piece, ref)
                if onward:
                    yield [k]
                    ref = place(lax.rem(base + 8, 16), piece)
                    arrived(k, ref)
                    to_sibling(base, 8, piece, ref)

            plan.spawn(take(kr, 12, part == 0 and not direct, xp, "x+"))
            plan.spawn(take(kl, 4, part == 1 and not direct, xm, "x-"))
            if direct:
                plan.spawn(take(kf, 8, False, None, None))
            to_sibling(base, 0, piece, ref)

        def far(k, piece, direct):
            yield [k]
            arrived(k, place(s_yh, piece))
            across(s_yh, piece, place(s_yh, piece), direct)

        def far_piece(piece, direct):
            k = send(mine(piece), place(s, piece), dev_yh if piece[0] == 0 else dev_yh1, "y", kib(piece))
            plan.spawn(far(k, piece, direct))
            return k

        def swapped():
            yield [swap]
            arrived(swap, place(s, (1, 0, rows)))
            across(s, (1, 0, rows), place(s, (1, 0, rows)), False)

        def later(pieces, k):
            for i, piece in enumerate(pieces):
                if FAR_AFTER:
                    yield [("sent", k)]
                    sent(k)
                k = far_piece(piece, FAR_DIRECT and i == len(pieces) - 1)
            yield [0.0]

        n = rows // FAR_SPLIT if key == "w" else rows
        pieces = [(part, r0, n) for part in (0, 1) for r0 in range(0, rows, n)]
        swap = send(mine((1, 0, rows)), place(s, (1, 0, rows)), dev_c1, "c1", kib((1, 0, rows)))
        first = far_piece(pieces[0], False)
        local.start()
        across(s, (0, 0, rows), mine((0, 0, rows)), False)
        plan.spawn(swapped())
        plan.spawn(later(pieces[1:], first))

    def scaled(r0, nr, block):
        column = pl.multiple_of(block * 256, 256)
        row_gain = gain[:, pl.ds(pl.multiple_of(block * 512 + kappa * 256, 256), 256)]
        fresh = r0 not in begun
        begun.add(r0)

        @pl.loop(0, nr // 16)
        def _(i):
            rows = pl.ds(pl.multiple_of(r0 + i * 16, 16), 16)
            x = xr[block, rows, :].astype(F32)
            total = x[:, :128] * x[:, :128] + x[:, 128:] * x[:, 128:]
            xn[rows, pl.ds(column, 256)] = (x * row_gain).astype(BF16)
            ssq[rows, :] = total if fresh else ssq[rows, :] + total

        plan.busy(nr / 900)

    begun = set()

    def squares(chunk):
        r0, r1 = CHUNKS[chunk]
        ssend[chunk, :, 0 : r1 - r0] = lax.dot_general(
            jnp.ones((8, 128), F32), ssq[r0:r1, :], (((1,), (1,)), ((), ())),
            precision=lax.Precision.HIGHEST, preferred_element_type=F32,
        )
        plan.busy(0.2)

    def product(chunk, half):
        r0, r1 = CHUNKS[chunk]
        cols = slice(half * 384, half * 384 + 384)
        acc[r0:r1, :] = jnp.dot(xn[r0:r1, 0:1024], panel[0:1024, cols], preferred_element_type=F32)

        @pl.loop(1, 4)
        def _(k):
            depth = pl.ds(pl.multiple_of(k * 1024, 1024), 1024)
            acc[r0:r1, :] += jnp.dot(xn[r0:r1, depth], panel[depth, cols], preferred_element_type=F32)

        plan.busy(0.4 + (r1 - r0) / 320)

    def combine(chunk):
        r0, r1 = CHUNKS[chunk]
        nr = r1 - r0
        both = ssend[chunk, :, 0:nr] + srecv[chunk, :, 0:nr]
        eye = (lax.broadcasted_iota(jnp.int32, (nr, nr), 0) == lax.broadcasted_iota(jnp.int32, (nr, nr), 1)).astype(F32)
        column = lax.dot_general(
            eye, both, (((1,), (1,)), ((), ())), precision=lax.Precision.HIGHEST, preferred_element_type=F32
        )[:, 0:1]
        scale = lax.rsqrt(column * (1.0 / 8192.0) + 1e-06)
        total = acc[r0:r1, :] + precv[r0:r1, :].astype(F32)
        feats[r0 + HALO : r1 + HALO, :] = total * scale
        plan.busy(nr / 250)

    def gated_rows(chunk):
        r0, r1 = CHUNKS[chunk]
        return (r0 + 16 if r0 else 0), (r1 + 16 if chunk else SLAB)

    def gates(chunk):
        t0, t1 = gated_rows(chunk)
        nr, e0 = t1 - t0, t0 + HALO

        def filtered(i, begin, rows):
            value = jnp.zeros((rows, 128), F32)
            for lag in range(3):
                value = value + pre[lag, i : i + 1, :] * feats[begin - lag : begin - lag + rows, i * 128 : i * 128 + 128]
            return value

        kv[e0 - 8 : e0 + nr, :] = filtered(1, e0 - 8, nr + 8) * filtered(2, e0 - 8, nr + 8)
        value = jnp.zeros((nr, 128), F32)
        for lag in range(7):
            value = value + inner[lag : lag + 1, :] * kv[e0 - lag : e0 - lag + nr, :]
        block = pl.multiple_of((2 * z + high) * 128, 128)
        gat[t0:t1, pl.ds(block, 128)] = (filtered(0, e0, nr) * value).astype(BF16)
        plan.busy(nr / 200)

    def product_out(chunk, half):
        t0, t1 = gated_rows(chunk)
        cols = slice(half * 256, half * 256 + 256)
        plan.busy(0.3 + (t1 - t0) / 600)
        return jnp.dot(gat[t0:t1, :], panel_out[:, cols], preferred_element_type=F32)

    def x_view(r0, r1):
        return lambda block: xr.at[block, pl.ds(r0, r1 - r0), :]

    def g_view(t0, t1):
        return lambda block: gat.at[pl.ds(t0, t1 - t0), pl.ds(pl.multiple_of(block * 128, 128), 128)]

    halo, stores = [], []

    def tokens_of(i):
        r0, r1 = TOKEN_ROWS[i]
        if i:
            yield [TOKEN_BEGIN[i]]
        gather(
            x_view(r0, r1), (r1 - r0) / 2, lambda block: scaled(r0, r1 - r0, block), f"x{r0}", TREES[TOKEN_TREE[i]]
        )
        yield [0.0]

    def compute(chunk):
        r0, r1 = CHUNKS[chunk]
        t0, t1 = gated_rows(chunk)
        yield [f"x{a}" for a, b in TOKEN_ROWS if r0 <= a < r1]
        squares(chunk)
        k2 = send(ssend.at[chunk], srecv.at[chunk], dev_c1, "c1", 12)
        yield ["w"]
        product(chunk, 1)
        psend[r0:r1, :] = acc[r0:r1, :].astype(BF16)
        k1 = send(psend.at[pl.ds(r0, r1 - r0), :], precv.at[pl.ds(r0, r1 - r0), :], dev_c1, "c1", (r1 - r0) * 0.75)
        yield [0.0]
        product(chunk, 0)
        yield [k1, k2] + [f"f{i}" for i in range(chunk)]
        arrived(k2, srecv.at[chunk])
        arrived(k1, precv.at[pl.ds(r0, r1 - r0), :])
        combine(chunk)
        plan.flags.add(f"f{chunk}")
        if chunk == 0:
            halo.append(send(feats.at[pl.ds(EXT - 8, 8), :], edge, dev_next, "c1", 12))
        if r0 == 0:
            yield [halo[0]]
            arrived(halo[0], edge)
            feats[8:16, :] = jnp.where(s == 0, 0.0, edge[...])
        gates(chunk)
        gather(g_view(t0, t1), (t1 - t0) / 4, lambda block: None, f"g{chunk}", TREES[GATED_TREE[chunk]])
        yield [f"g{chunk}", "wo"]
        osend[t0:t1, :] = product_out(chunk, 1).astype(BF16)
        k3 = send(osend.at[pl.ds(t0, t1 - t0), :], orecv.at[pl.ds(t0, t1 - t0), :], dev_c1, "c1", (t1 - t0) / 2)
        yield [0.0]
        acc2[t0:t1, :] = product_out(chunk, 0)
        yield [k3]
        arrived(k3, orecv.at[pl.ds(t0, t1 - t0), :])
        out[t0:t1, :] = (acc2[t0:t1, :] + orecv[t0:t1, :].astype(F32)).astype(BF16)
        store = pltpu.make_async_copy(out.at[pl.ds(t0, t1 - t0), :], out_hbm.at[pl.ds(t0, t1 - t0), :], store_sem.at[chunk])
        store.start()
        stores.append(store)
        plan.busy((t1 - t0) / 1000)

    def out_weights():
        yield [WO_BEGIN]
        weights(wo, panel_out, 128, 256, "wo", local_sem.at[1])

    plan.spawn(tokens_of(0))
    weights(wf, panel, 256, 384, "w", local_sem.at[0])
    for i in range(1, len(TOKEN_ROWS)):
        plan.spawn(tokens_of(i))
    plan.spawn(out_weights())
    for chunk in range(len(CHUNKS)):
        plan.spawn(compute(chunk), 2 + chunk)
    plan.run()
    for store in stores:
        store.wait()
    for k in range(len(started)):
        sent(k)
    assert len(started) <= N_RECV, len(started)


def on_device(tokens, norm_gain, w_feat, pre_taps, inner_taps, w_out):
    hbm = pl.BlockSpec(memory_space=pl.ANY)
    return pl.pallas_call(
        body,
        out_shape=jax.ShapeDtypeStruct((SLAB, 256), BF16),
        in_specs=[hbm] * 6,
        out_specs=hbm,
        scratch_shapes=[
            pltpu.VMEM((1, 8192), F32),
            pltpu.VMEM((3, 3, 128), F32),
            pltpu.VMEM((7, 128), F32),
            pltpu.VMEM((256, 256), BF16),
            pltpu.VMEM((SLAB, 256), BF16),
            pltpu.VMEM((SLAB, 384), BF16),
            pltpu.VMEM((16, SLAB, 256), BF16),
            pltpu.VMEM((SLAB, 4096), BF16),
            pltpu.VMEM((4096, 768), BF16),
            pltpu.VMEM((2048, 512), BF16),
            pltpu.VMEM((SLAB, 384), F32),
            pltpu.VMEM((SLAB, 384), BF16),
            pltpu.VMEM((SLAB, 384), BF16),
            pltpu.VMEM((EXT, 384), F32),
            pltpu.VMEM((8, 384), F32),
            pltpu.VMEM((EXT, 128), F32),
            pltpu.VMEM((SLAB, 128), F32),
            pltpu.VMEM((len(CHUNKS), 8, 384), F32),
            pltpu.VMEM((len(CHUNKS), 8, 384), F32),
            pltpu.VMEM((SLAB, 2048), BF16),
            pltpu.VMEM((SLAB, 256), F32),
            pltpu.VMEM((SLAB, 256), BF16),
            pltpu.VMEM((SLAB, 256), BF16),
            pltpu.SemaphoreType.DMA((N_SEND,)),
            pltpu.SemaphoreType.DMA((N_RECV,)),
            pltpu.SemaphoreType.DMA((2,)),
            pltpu.SemaphoreType.DMA((8,)),
            pltpu.SemaphoreType.DMA((len(CHUNKS),)),
        ],
        compiler_params=pltpu.CompilerParams(
            collective_id=0, has_side_effects=True, vmem_limit_bytes=56 * 1024 * 1024
        ),
    )(
        tokens,
        norm_gain.reshape(1, 8192),
        jnp.moveaxis(w_feat, 1, 0),
        pre_taps,
        inner_taps,
        w_out,
    )


def solution(mesh):
    in_specs = (
        P("seq", ("fsdp", "chan")),
        P(),
        P("seq", None, ("fsdp", "chan")),
        P(None, None, ("fsdp", "chan")),
        P(None, ("fsdp", "chan")),
        P("seq", ("fsdp", "chan")),
    )
    out_specs = P("seq", ("fsdp", "chan"))
    return jax.shard_map(
        on_device, mesh=mesh, in_specs=in_specs, out_specs=out_specs, check_vma=False
    )
```

time: 582 us -> 103 us (0.18)
  waiting for transfers between devices: 539 us -> 0 us
  Pallas kernels: 0 us -> 99.6 us
  matrix products: 14.6 us -> 0 us
  between operations: 13.2 us -> 0.01 us
  other arithmetic: 7.11 us -> 0 us
    all_gather x4 -> x0, waiting for transfers between devices: 521 us -> none  [the longest x1 223 us: on_device(): gathered = lax.all_gather(tokens, ('fsdp', 'chan'), axis=1, tiled=True)]
    pallas_call x0 -> x1, Pallas kernels: none -> 99.6 us  [on_device(): pl.pallas_call(body, out_shape=jax.ShapeDtypeStruct((SLAB, 256), BF16), i...]
    ppermute x2 -> x0, waiting for transfers between devices: 16.9 us -> none  [passed_along(): lax.ppermute(value, axis, [(source, source + steps) for source in range(f...]
    dot_general x2 -> x0, matrix products: 14.6 us -> none  [the longest x1 9.72 us: on_device(): accum = jnp.dot(columns, flat_piece, preferred_element_type=jnp.float32)]
  transfers between devices with their start and end apart: 6 -> 0, of which waited for: 6 -> 0; matrix products, arithmetic and copies ran while one was open for 3% -> 0% of each run, Pallas kernels for 0% -> 0%
where the time goes in v2:
time: 103 us; the launch traced here: 101 us
  Pallas kernels  99.6 us (97%)
  local copies, waits for them, and re-layouts  1.67 us (2%)
    pallas_call x1, Pallas kernels, on_device(): pl.pallas_call(body, out_shape=jax.ShapeDtypeStruct((SLAB, 256), BF16), i...  99.6 us

profile of v2, /device:TPU:6, one launch (start us, length us, event | category | flops | bytes accessed | tf_op | source)
XLA Modules:
  0.0 101.2 jit_solution(2189937136743766655)
XLA Ops:
  0.0 99.6 %shard_map.64 = bf16[512,256]{1,0:T(8,128)(2,1)} custom-call(bf16[512,256]{1,0:T(8,128)(2,1)} %tok_hbm.1, f32[1,8192]{1,0:T(1,128)} %bitcast.3, bf16[3,512,128]{2,1,0:T(8,128)(2,1)} %bitcast.2, f32[3,3,128]{2,1,0:T(4,128)} %pre_hbm.1, f32[7,128]{1,0:T(8,128)} %inner_hbm.1, bf16[256,256]{1,0:T(8,128)(2,1)} %wo_hbm.1), custom_call_target="tpu_custom_call" | custom-call | tf_op jit(solution)/shard_map/pallas_call | solution.py:462
  99.6 1.7 %copy.8 = bf16[512,256]{1,0:T(8,128)(2,1)} copy(bf16[512,256]{1,0:T(8,128)(2,1)} %shard_map.64) | data formatting | bytes 524288

commit v3 on v2

--- a/solution.py
+++ b/solution.py
@@ -12,9 +12,10 @@
 TOKEN_ROWS = ((384, 512), (256, 384), (128, 256), (0, 128))
 CHUNKS = ((384, 512), (256, 384), (128, 256), (0, 128))
 RATE = {"z+": 45.0, "z-": 45.0, "x+": 45.0, "x-": 45.0, "y": 22.5, "c1": 45.0, "core": 400.0}
-LATENCY = 2.8
+LATENCY = {"z+": 2.8, "z-": 2.8, "x+": 2.8, "x-": 2.8, "y": 2.8, "c1": 2.8, "core": 2.8}
 FAIR = ("y", "c1")
 TOKEN_BEGIN = (0.0, 1.6, 5.3, 26.8)
+TOKEN_TURN = (0.0, 0.0, 0.0, 0.0)
 RIGHT, LEFT = {(1, 0): [(2, 0)], (2, 0): [(3, 0)], (3, 0): [(4, 0)]}, {(-1, 0): [(-2, 0)], (-2, 0): [(-3, 0)]}
 OTHER = {(1, 1): [(2, 1)], (2, 1): [(3, 1)], (-1, 1): [(-2, 1)], (-2, 1): [(-3, 1)], (-3, 1): [(-4, 1)]}
 SKIP = {
@@ -27,12 +28,25 @@
     "diag": {(0, 0): [(1, 0), (-1, 0), (-1, 1), (1, 1), (0, 1)], **RIGHT, **LEFT, **OTHER},
     "skip": {(0, 0): [(0, 1), (1, 0), (-1, 0)], (0, 1): [(-1, 1), (1, 1)], **SKIP},
     "fast": {(0, 0): [(1, 0), (-1, 1), (-1, 0), (1, 1), (0, 1)], **SKIP},
+    "ydia": {
+        (0, 0): [(1, 0), (-1, 0), (-1, 1), (1, 1), (0, 1)], **RIGHT, **LEFT, **OTHER_Y,
+    },
+    "late": {(0, 0): [(1, 0), (-1, 0), (0, 1)], (0, 1): [(-1, 1), (1, 1)], **RIGHT, **LEFT, **OTHER},
     "viay": {(0, 0): [(0, 1), (1, 0), (-1, 0)], (0, 1): [(-1, 1), (1, 1)], **RIGHT, **LEFT, **OTHER_Y},
+}
+TREES["all"] = {(0, 0): [(d, side) for d in (4, 1, -1, 2, -2, 3, -3) for side in (0, 1)] + [(0, 1)]}
+TREES["half"] = {(0, 0): [(0, 1)] + [(d, 0) for d in (4, 1, -1, 2, -2, 3, -3)], (0, 1): [(d, 1) for d in (-4, 1, -1, 2, -2, 3, -3)]}
+TREES["duo"] = {
+    (0, 0): [(0, 1), (2, 0), (-2, 0), (1, 0), (-1, 0)], (2, 0): [(4, 0), (3, 0)], (-2, 0): [(-3, 0)],
+    (0, 1): [(-2, 1), (2, 1), (1, 1), (-1, 1)], (-2, 1): [(-4, 1), (-3, 1)], (2, 1): [(3, 1)],
 }
 TOKEN_TREE = ("ring", "viay", "ring", "skip")
 GATED_TREE = ("ring", "diag", "viay", "fast")
 WO_BEGIN = 33.0
 FAR_AFTER = True
+W_FIRST = False
+LEAF_SLACK = 1.5
+WO_SPLIT = 1
 FAR_SPLIT = 2
 FAR_DIRECT = True
 
@@ -56,7 +70,7 @@
             self.order += 1
             key = -self.order
         self.flows.append([key, link, float(kib)])
-        self.clock_to(self.clock + 0.08)
+        self.clock_to(self.clock + 0.12)
 
     def busy(self, us):
         self.clock_to(self.clock + us)
@@ -82,7 +96,7 @@
             for flow in [f for f in self.flows if f[2] <= 1e-6]:
                 self.flows.remove(flow)
                 self.left[flow[0]] = self.clock + 0.3
-                self.landed[flow[0]] = self.clock + LATENCY
+                self.landed[flow[0]] = self.clock + LATENCY[flow[1]]
             if self.clock >= until - 1e-9:
                 return
 
@@ -92,7 +106,8 @@
         if isinstance(need, str):
             return 0.0 if need in self.flags else None
         if isinstance(need, tuple):
-            return self.left.get(need[1])
+            times, more = (self.left, 0.0) if need[0] == "sent" else (self.landed, LEAF_SLACK)
+            return times[need[1]] + more if need[1] in times else None
         return self.landed.get(need)
 
     def run(self):
@@ -188,29 +203,39 @@
     def block_of(steps, hi):
         return 2 * lax.rem(z + steps + 8, 8) + hi
 
-    def gather(view, kib, use, flag, tree):
+    def gather(view, kib, use, flag, tree, turn_at=0.0):
         count = [0]
 
         def holder(node):
             return block_of(-node[0], high if node[1] == 0 else 1 - high)
 
+        def hand(node, child):
+            steps, turn = child[0] - node[0], child[1] != node[1]
+            dev = (s, lax.rem(z + steps + 8, 8), c2 if turn else c)
+            link = "z+" if steps > 0 else "z-"
+            if turn and steps:
+                plan.start(None, link, kib)
+            ref = view(holder(node))
+            k = send(ref, ref, dev, "y" if turn else link, kib * (1 if turn else abs(steps)))
+            plan.spawn(take(child, k))
+
+        def turn_later(child):
+            yield [turn_at]
+            hand((0, 0), child)
+
         def pass_on(node):
-            ref = view(holder(node))
             for child in tree.get(node, ()):
-                steps, turn = child[0] - node[0], child[1] != node[1]
-                dev = (s, lax.rem(z + steps + 8, 8), c2 if turn else c)
-                link = "z+" if steps > 0 else "z-"
-                if turn and steps:
-                    plan.start(None, link, kib)
-                k = send(ref, ref, dev, "y" if turn else link, kib * (1 if turn else abs(steps)))
-                plan.spawn(take(child, k))
+                if turn_at and node == (0, 0) and child[1]:
+                    plan.spawn(turn_later(child))
+                else:
+                    hand(node, child)
             use(holder(node))
             count[0] += 1
             if count[0] == 16:
                 plan.flags.add(flag)
 
         def take(node, k):
-            yield [k]
+            yield [k if node in tree else ("leaf", k)]
             arrived(k, view(holder(node)))
             pass_on(node)
 
@@ -229,21 +254,22 @@
         def kib(piece):
             return piece[2] * cols * 2 / 1024
 
-        rest = [2 * 16 * rows]
+        rest, sib = [16 * rows], []
         local = pltpu.make_async_copy(mine((0, 0, rows)), place(s, (0, 0, rows)), sem)
 
         def to_sibling(base, far, piece, ref):
             k = send(ref, place(lax.rem(base + far, 16), piece), dev_sib, "core", kib(piece))
-
-            def take():
-                yield [k]
-                arrived(k, place(lax.rem(base + 1 - 2 * core + far, 16), piece))
-                rest[0] -= 2 * piece[2]
-                if not rest[0]:
-                    local.wait()
-                    plan.flags.add(key)
-
-            plan.spawn(take(), 1)
+            sib.append((k, place(lax.rem(base + 1 - 2 * core + far, 16), piece)))
+            rest[0] -= piece[2]
+            if not rest[0]:
+                plan.spawn(finish(), 1)
+
+        def finish():
+            yield [k for k, _ in sib]
+            for k, ref in sib:
+                arrived(k, ref)
+            local.wait()
+            plan.flags.add(key)
 
         def across(base, piece, ref, direct):
             part = piece[0]
@@ -295,7 +321,7 @@
                 k = far_piece(piece, FAR_DIRECT and i == len(pieces) - 1)
             yield [0.0]
 
-        n = rows // FAR_SPLIT if key == "w" else rows
+        n = rows // (FAR_SPLIT if key == "w" else WO_SPLIT)
         pieces = [(part, r0, n) for part in (0, 1) for r0 in range(0, rows, n)]
         swap = send(mine((1, 0, rows)), place(s, (1, 0, rows)), dev_c1, "c1", kib((1, 0, rows)))
         first = far_piece(pieces[0], False)
@@ -318,7 +344,7 @@
             xn[rows, pl.ds(column, 256)] = (x * row_gain).astype(BF16)
             ssq[rows, :] = total if fresh else ssq[rows, :] + total
 
-        plan.busy(nr / 900)
+        plan.busy(nr / 2500)
 
     begun = set()
 
@@ -328,19 +354,14 @@
             jnp.ones((8, 128), F32), ssq[r0:r1, :], (((1,), (1,)), ((), ())),
             precision=lax.Precision.HIGHEST, preferred_element_type=F32,
         )
-        plan.busy(0.2)
+        plan.busy(0.3)
 
     def product(chunk, half):
         r0, r1 = CHUNKS[chunk]
         cols = slice(half * 384, half * 384 + 384)
-        acc[r0:r1, :] = jnp.dot(xn[r0:r1, 0:1024], panel[0:1024, cols], preferred_element_type=F32)
-
-        @pl.loop(1, 4)
-        def _(k):
-            depth = pl.ds(pl.multiple_of(k * 1024, 1024), 1024)
-            acc[r0:r1, :] += jnp.dot(xn[r0:r1, depth], panel[depth, cols], preferred_element_type=F32)
-
-        plan.busy(0.4 + (r1 - r0) / 320)
+        acc[r0:r1, :] = jnp.dot(xn[r0:r1, :], panel[:, cols], preferred_element_type=F32)
+
+        plan.busy(0.35 + (r1 - r0) / 200)
 
     def combine(chunk):
         r0, r1 = CHUNKS[chunk]
@@ -353,7 +374,7 @@
         scale = lax.rsqrt(column * (1.0 / 8192.0) + 1e-06)
         total = acc[r0:r1, :] + precv[r0:r1, :].astype(F32)
         feats[r0 + HALO : r1 + HALO, :] = total * scale
-        plan.busy(nr / 250)
+        plan.busy(0.1 + nr / 2000)
 
     def gated_rows(chunk):
         r0, r1 = CHUNKS[chunk]
@@ -375,12 +396,12 @@
             value = value + inner[lag : lag + 1, :] * kv[e0 - lag : e0 - lag + nr, :]
         block = pl.multiple_of((2 * z + high) * 128, 128)
         gat[t0:t1, pl.ds(block, 128)] = (filtered(0, e0, nr) * value).astype(BF16)
-        plan.busy(nr / 200)
+        plan.busy(0.05 + nr / 3000)
 
     def product_out(chunk, half):
         t0, t1 = gated_rows(chunk)
         cols = slice(half * 256, half * 256 + 256)
-        plan.busy(0.3 + (t1 - t0) / 600)
+        plan.busy(0.1 + (t1 - t0) / 2000)
         return jnp.dot(gat[t0:t1, :], panel_out[:, cols], preferred_element_type=F32)
 
     def x_view(r0, r1):
@@ -393,10 +414,10 @@
 
     def tokens_of(i):
         r0, r1 = TOKEN_ROWS[i]
-        if i:
+        if TOKEN_BEGIN[i]:
             yield [TOKEN_BEGIN[i]]
         gather(
-            x_view(r0, r1), (r1 - r0) / 2, lambda block: scaled(r0, r1 - r0, block), f"x{r0}", TREES[TOKEN_TREE[i]]
+            x_view(r0, r1), (r1 - r0) / 2, lambda block: scaled(r0, r1 - r0, block), f"x{r0}", TREES[TOKEN_TREE[i]], TOKEN_TURN[i]
         )
         yield [0.0]
 
@@ -442,8 +463,11 @@
         yield [WO_BEGIN]
         weights(wo, panel_out, 128, 256, "wo", local_sem.at[1])
 
-    plan.spawn(tokens_of(0))
+    if not W_FIRST:
+        plan.spawn(tokens_of(0))
     weights(wf, panel, 256, 384, "w", local_sem.at[0])
+    if W_FIRST:
+        plan.spawn(tokens_of(0))
     for i in range(1, len(TOKEN_ROWS)):
         plan.spawn(tokens_of(i))
     plan.spawn(out_weights())

time: 103 us -> 101 us (0.981); the launches traced: 101 us -> 101 us
  no operation moved by 1% of the time
where the time goes in v3:
time: 101 us
  Pallas kernels  99.1 us (98%)
  local copies, waits for them, and re-layouts  1.67 us (2%)
    pallas_call x1, Pallas kernels, on_device(): pl.pallas_call(body, out_shape=jax.ShapeDtypeStruct((SLAB, 256), BF16), i...  99.1 us

profile of v3, /device:TPU:6, one launch (start us, length us, event | category | flops | bytes accessed | tf_op | source)
XLA Modules:
  0.0 100.8 jit_solution(6220558389834736997)
XLA Ops:
  0.0 99.1 %shard_map.64 = bf16[512,256]{1,0:T(8,128)(2,1)} custom-call(bf16[512,256]{1,0:T(8,128)(2,1)} %tok_hbm.1, f32[1,8192]{1,0:T(1,128)} %bitcast.3, bf16[3,512,128]{2,1,0:T(8,128)(2,1)} %bitcast.2, f32[3,3,128]{2,1,0:T(4,128)} %pre_hbm.1, f32[7,128]{1,0:T(8,128)} %inner_hbm.1, bf16[256,256]{1,0:T(8,128)(2,1)} %wo_hbm.1), custom_call_target="tpu_custom_call" | custom-call | tf_op jit(solution)/shard_map/pallas_call | solution.py:486
  99.1 1.7 %copy.8 = bf16[512,256]{1,0:T(8,128)(2,1)} copy(bf16[512,256]{1,0:T(8,128)(2,1)} %shard_map.64) | data formatting | bytes 524288
